TPU v7x, 32 devices: a whole 2x2x4 slice. The times are simulated.
32 devices in a mesh: dp: 8 (over y, x, core), expert: 4 (over z).
Axes of the slice: x: 2, y: 2, z: 4, core: 2. Of those that a mesh axis runs over, the one named last changes fastest.
Arguments:
- residual: bfloat16 [4096, 2048], P(('dp', 'expert')), may hold values from -6 to 6
- grad_stream: bfloat16 [4096, 2048], P(('dp', 'expert')), may hold values from -6 to 6
- expert_gain: float32 [2048], replicated, may hold values from 0.5 to 1.5
- router_weight: bfloat16 [2048, 32], replicated, may hold values from -0.125 to 0.125
- gate_up_weight: bfloat16 [32, 2048, 1536], P('expert', 'dp'), may hold values from -0.125 to 0.125
- down_weight: bfloat16 [32, 2048, 768], P('expert', 'dp'), may hold values from -0.21875 to 0.21875
- need_lists: int32 [4, 2], replicated, may hold values from 0 to 31, as said below
- routes: int32 [4096, 1], P(('dp', 'expert')), may hold values from 0 to 1
Outputs:
- stream: bfloat16 [4096, 2048], P(('dp', 'expert'))
- grad_residual: bfloat16 [4096, 2048], P(('dp', 'expert'))
Inputs may be any that keep to these rules, and one draw needn't show every extreme that they name: `need_lists`: row c lists 2 experts with different owner indices (expert id // 8).
All inputs are finite; a program needn't handle non-finite values.
Results may differ from a plain program's by a relative error of at most 0.008.
Values may be sent and summed in bfloat16 or wider, within the bound.
A program may use at most 128 MiB of HBM per device.

v0:
```python
import jax
import jax.numpy as jnp
from jax import lax
from jax.sharding import PartitionSpec as P

eps = 1e-05


def partner(value, axis, stride):
    mask = 2**stride
    pairs = [(source, source ^ mask) for source in range(lax.axis_size(axis))]
    return lax.ppermute(value, axis, pairs)


def norm_factor(values):
    return lax.rsqrt(jnp.mean(values * values, axis=-1, keepdims=True) + eps)


def norm_backward(values, factor, gain, grad):
    scaled = gain * grad
    return factor * scaled - values * factor**3 * jnp.mean(values * scaled, axis=-1, keepdims=True)


def body(
    residual,
    grad_stream,
    expert_gain,
    router_weight,
    gate_up_weight,
    down_weight,
    need_lists,
    routes,
):
    column = lax.axis_index("expert")
    ranks = lax.axis_size("dp")
    parity = lax.axis_index("dp") % 2
    held = gate_up_weight.shape[0]
    width = down_weight.shape[2]
    tokens = residual.shape[0]
    listed = lax.dynamic_index_in_dim(need_lists, column, 0, keepdims=False)
    owner_of = need_lists // held
    local_of = need_lists % held
    mine = owner_of == column
    has_one = jnp.any(mine, axis=1)
    local_pick = jnp.sum(jnp.where(mine, local_of, 0), axis=1)
    owned = jnp.stack(
        [gate_up_weight[:, :, :width], gate_up_weight[:, :, width:], down_weight], axis=2
    )
    outgoing = jnp.where(
        has_one[:, None, None, None],
        jnp.take(owned, local_pick, axis=0),
        jnp.zeros((), jnp.bfloat16),
    )
    arrived = lax.all_to_all(outgoing, "expert", split_axis=0, concat_axis=0, tiled=True)
    slot_rows = jnp.take(arrived, listed // held, axis=0)
    spread_out = jnp.broadcast_to(slot_rows[None], (ranks // 2,) + slot_rows.shape).reshape(
        (ranks,) + slot_rows.shape[1:]
    )
    stream_in = residual.astype(jnp.float32)
    factor_in = norm_factor(stream_in)
    normed = (stream_in * factor_in * expert_gain).astype(jnp.bfloat16)
    router_cols = jnp.take(router_weight, listed, axis=1)
    logits = jnp.dot(normed, router_cols, preferred_element_type=jnp.float32)
    gates = jax.nn.sigmoid(logits - logits[:, ::-1])
    select = (routes == jnp.arange(2, dtype=jnp.int32)[None, :]).astype(jnp.float32)
    mix = gates * select
    mix_here = lax.dynamic_index_in_dim(mix, parity, 1, keepdims=False)
    mix_there = lax.dynamic_index_in_dim(mix, 1 - parity, 1, keepdims=False)
    grad_out = grad_stream.astype(jnp.float32)
    send_grad = (mix_there[:, None] * grad_out).astype(jnp.bfloat16)
    partner_normed, partner_grad = partner((normed, send_grad), "dp", 0)
    pair_normed = jnp.concatenate([normed, partner_normed], axis=0)
    weights = lax.all_to_all(spread_out, "dp", split_axis=0, concat_axis=1, tiled=True)[0]
    hidden = jnp.einsum(
        "td,dkf->tkf", pair_normed, weights[:, :2], preferred_element_type=jnp.float32
    )
    gate_part = hidden[:, 0]
    up_part = hidden[:, 1]
    sigma = jax.nn.sigmoid(gate_part)
    silu_gate = gate_part * sigma
    act = (silu_gate * up_part).astype(jnp.bfloat16)
    branch = jnp.einsum("tf,df->td", act, weights[:, 2], preferred_element_type=jnp.float32).astype(
        jnp.bfloat16
    )
    other_branch = partner(branch[tokens:], "dp", 0)
    branch_here = branch[:tokens].astype(jnp.float32)
    branch_there = other_branch.astype(jnp.float32)
    stream = (
        stream_in + mix_here[:, None] * branch_here + mix_there[:, None] * branch_there
    ).astype(jnp.bfloat16)
    mix_grad_here = jnp.sum(branch_here * grad_out, axis=-1)
    mix_grad_there = jnp.sum(branch_there * grad_out, axis=-1)
    grad_mix = jnp.where(
        parity == 0,
        jnp.stack([mix_grad_here, mix_grad_there], axis=1),
        jnp.stack([mix_grad_there, mix_grad_here], axis=1),
    )
    grad_branch = jnp.concatenate(
        [(mix_here[:, None] * grad_out).astype(jnp.bfloat16), partner_grad], axis=0
    )
    grad_act = jnp.einsum(
        "td,df->tf", grad_branch, weights[:, 2], preferred_element_type=jnp.float32
    )
    slope = sigma * (1.0 + gate_part * (1.0 - sigma))
    grad_hidden = jnp.stack([grad_act * up_part * slope, grad_act * silu_gate], axis=1).astype(
        jnp.bfloat16
    )
    expert_term = jnp.einsum(
        "tkf,dkf->td", grad_hidden, weights[:, :2], preferred_element_type=jnp.float32
    ).astype(jnp.bfloat16)
    other_term = partner(expert_term[tokens:], "dp", 0)
    grad_gates = grad_mix * select
    grad_logits = (
        gates * (grad_gates - jnp.sum(gates * grad_gates, axis=-1, keepdims=True))
    ).astype(jnp.bfloat16)
    grad_normed = expert_term[:tokens].astype(jnp.float32) + other_term.astype(jnp.float32)
    grad_normed = grad_normed + jnp.einsum(
        "tn,dn->td", grad_logits, router_cols, preferred_element_type=jnp.float32
    )
    grad_residual = (
        grad_out + norm_backward(stream_in, factor_in, expert_gain, grad_normed)
    ).astype(jnp.bfloat16)
    return (stream, grad_residual)


def solution(mesh):
    return jax.shard_map(
        body,
        mesh=mesh,
        in_specs=(
            P(("dp", "expert"), None),
            P(("dp", "expert"), None),
            P(),
            P(),
            P("expert", "dp", None),
            P("expert", "dp", None),
            P(),
            P(("dp", "expert"), None),
        ),
        out_specs=(P(("dp", "expert"), None), P(("dp", "expert"), None)),
        check_vma=False,
    )
```

profile of v0, /device:TPU:0, one launch (start us, length us, event | category | flops | bytes accessed | tf_op | source)
XLA Modules:
  0.0 289.3 jit_solution(1580183164395549183)
XLA Ops:
  0.6 0.7 fusion.64
  1.4 0.7 fusion.49
  2.1 5.0 %slice_bitcast_fusion.2 = (bf16[8,256,1,768]{3,1,0,2:T(8,128)(2,1)S(1)}, bf16[8,256,1,768]{3,1,0,2:T(8,128)(2,1)}) fusion(bf16[8,256,1536]{2,1,0:T(8,128)(2,1)} %param.12), kind=kLoop, calls=%fused_computation.11 | loop fusion | bytes 12582912 | tf_op jit(solution)/shard_map/stack | solution.py:46
  7.1 7.0 %pad_maximum_fusion = bf16[8,256,3,768]{3,1,0,2:T(8,128)(2,1)} fusion(bf16[8,256,1,768]{3,1,0,2:T(8,128)(2,1)} %bitcast.97, bf16[8,256,1,768]{3,1,0,2:T(8,128)(2,1)} %get-tuple-element.9, bf16[8,256,1,768]{3,1,0,2:T(8,128)(2,1)S(1)} %get-tuple-element.8), kind=kLoop, calls=%fused_computation.3 | loop fusion | flops 9437184 | bytes 18874368 | tf_op jit(solution)/shard_map/stack | solution.py:46
  14.1 6.8 %gather_fusion.1 = bf16[4,256,3,768]{3,1,2,0:T(8,128)(2,1)} fusion(bf16[8,256,3,768]{3,1,0,2:T(8,128)(2,1)} %pad_maximum_fusion, s32[1024]{0:T(1024)S(1)} %pad_clamp_fusion.1), kind=kCustom, calls=%fused_computation.1 | custom fusion | bytes 9437200 | tf_op jit(solution)/shard_map/jit(_take)/gather | solution.py:51
  20.8 5.2 %select_select_fusion = bf16[4,256,3,768]{3,1,2,0:T(8,128)(2,1)} fusion(bf16[4,256,3,768]{3,1,2,0:T(8,128)(2,1)} %gather_fusion.1, pred[4]{0:T(512)(128)(4,1)S(1)} %compare_and_fusion, pred[4]{0:T(512)(128)(4,1)S(1)} %get-tuple-element.6), kind=kLoop, calls=%fused_computation.8 | loop fusion | flops 4718592 | bytes 9437192 | tf_op jit(solution)/shard_map/jit(_where)/select_n | solution.py:49
  26.0 6.4 %all-to-all-start = ((bf16[4,256,3,768]{3,1,2,0:T(8,128)(2,1)}), bf16[4,256,3,768]{3,1,2,0:T(8,128)(2,1)}, u32[]{:S(2)}, u32[]{:S(2)}) async-start(bf16[4,256,3,768]{3,1,2,0:T(8,128)(2,1)} %select_select_fusion), calls=%async_computation | async-start | bytes 9437184 | tf_op jit(solution)/shard_map/all_to_all | solution.py:54
  32.5 0.2 dynamic-slice_reduce_fusion
  32.7 104.5 %all-to-all-done = bf16[4,256,3,768]{3,1,2,0:T(8,128)(2,1)} async-done(((bf16[4,256,3,768]{3,1,2,0:T(8,128)(2,1)}), bf16[4,256,3,768]{3,1,2,0:T(8,128)(2,1)}, u32[]{:S(2)}, u32[]{:S(2)}) %all-to-all-start) | async-done | bytes 4718624 | tf_op jit(solution)/shard_map/all_to_all | solution.py:54
  137.2 3.0 %gather_fusion.2 = bf16[2,256,3,768]{3,1,2,0:T(8,128)(2,1)S(1)} fusion(bf16[4,256,3,768]{3,1,2,0:T(8,128)(2,1)} %all-to-all-done, s32[1024]{0:T(1024)S(1)} %pad_clamp_fusion), kind=kCustom, calls=%fused_computation.2 | custom fusion | bytes 4718600 | tf_op jit(solution)/shard_map/jit(_take)/gather | solution.py:55
  140.3 0.3 broadcast_select_fusion
  140.6 4.7 %broadcast_in_dim.69 = bf16[4,2,256,3,768]{4,2,3,1,0:T(8,128)(2,1)} broadcast(bf16[2,256,3,768]{3,1,2,0:T(8,128)(2,1)S(1)} %broadcast_select_fusion), dimensions={1,2,3,4} | broadcast | bytes 11796480 | tf_op jit(solution)/shard_map/broadcast_in_dim | solution.py:56
  145.3 5.2 %all-to-all-start.1 = ((bf16[8,256,3,768]{3,1,2,0:T(8,128)(2,1)}), bf16[8,256,3,768]{3,1,2,0:T(8,128)(2,1)}, u32[]{:S(2)}, u32[]{:S(2)}) async-start(bf16[8,256,3,768]{3,1,2,0:T(8,128)(2,1)} %bitcast.92), calls=%async_computation.1 | async-start | bytes 18874368 | tf_op jit(solution)/shard_map/all_to_all | solution.py:73
  150.5 0.2 fusion.15
  150.7 0.2 fusion.17
  150.9 0.4 collective-permute-start
  151.3 104.4 %all-to-all-done.1 = bf16[8,256,3,768]{3,1,2,0:T(8,128)(2,1)} async-done(((bf16[8,256,3,768]{3,1,2,0:T(8,128)(2,1)}), bf16[8,256,3,768]{3,1,2,0:T(8,128)(2,1)}, u32[]{:S(2)}, u32[]{:S(2)}) %all-to-all-start.1) | async-done | bytes 9437216 | tf_op jit(solution)/shard_map/all_to_all | solution.py:73
  255.8 8.2 %copy.11 = bf16[8,256,3,768]{3,1,0,2:T(8,128)(2,1)} copy(bf16[8,256,3,768]{3,1,2,0:T(8,128)(2,1)} %all-to-all-done.1) | data formatting | bytes 18874368 | tf_op jit(solution)/shard_map/all_to_all | solution.py:73
  264.0 4.6 %fusion.2 = f32[256,2,768]{2,0,1:T(8,128)S(1)} fusion(bf16[2048,3,768]{2,0,1:T(8,128)(2,1)} %bitcast.93, bf16[128,2048]{1,0:T(8,128)(2,1)S(1)} %collective-permute-done, bf16[128,2048]{1,0:T(8,128)(2,1)S(1)} %fusion.17), kind=kOutput, calls=%fused_computation.6 | convolution fusion | flops 1612709888 | bytes 8912896 | tf_op jit(solution)/shard_map/td,dkf->tkf/dot_general | solution.py:74
  268.6 3.5 %fusion.12 = bf16[256,2048]{1,0:T(8,128)(2,1)S(1)} fusion(bf16[2048,3,768]{2,0,1:T(8,128)(2,1)} %bitcast.94, f32[256,2,768]{2,0,1:T(8,128)S(1)} %fusion.2), kind=kOutput, calls=%fused_computation.16 | convolution fusion | flops 807010304 | bytes 5767168 | tf_op jit(solution)/shard_map/tf,df->td/dot_general | solution.py:82
  272.3 0.6 gather_fusion
  272.9 1.3 fusion.63
  274.2 0.3 fusion.24
  274.6 0.2 fusion.21
  274.9 0.5 collective-permute-start.2
  275.4 1.5 collective-permute-done.2
  276.9 3.4 %fusion.45 = (bf16[256,1,768]{2,0,1:T(8,128)(2,1)S(1)}, bf16[256,1,768]{2,0,1:T(8,128)(2,1)S(1)}) fusion(f32[256,2,768]{2,0,1:T(8,128)} %copy-done.7, bf16[2048,3,768]{2,0,1:T(8,128)(2,1)} %bitcast.95, bf16[128,2048]{1,0:T(8,128)(2,1)S(1)} %collective-permute-done.2, bf16[128,2048]{1,0:T(8,128)(2,1)S(1)} %get-tuple-element.14), kind=kOutput, calls=%fused_computation.69 | convolution fusion | flops 809959424 | bytes 6553600 | tf_op jit(solution)/shard_map/td,df->tf/dot_general | solution.py:101
  280.4 4.6 %fusion.9 = bf16[256,2048]{1,0:T(8,128)(2,1)S(1)} fusion(bf16[2048,3,768]{2,0,1:T(8,128)(2,1)} %bitcast.96, bf16[256,1,768]{2,0,1:T(8,128)(2,1)S(1)} %get-tuple-element.11, bf16[256,1,768]{2,0,1:T(8,128)(2,1)S(1)} %get-tuple-element.10), kind=kOutput, calls=%fused_computation.15 | convolution fusion | flops 1611530240 | bytes 8126464 | tf_op jit(solution)/shard_map/tkf,dkf->td/dot_general | solution.py:108
  285.0 0.4 collective-permute-start.3
  285.5 1.5 collective-permute-done.3
  287.0 0.5 fusion.20
  287.6 1.7 fusion.25
  (34 shorter events, 0.4 us)
Async XLA Ops:
  0.6 271.6 %copy-start = (bf16[2048,32]{0,1:T(8,128)(2,1)S(1)}, bf16[2048,32]{0,1:T(8,128)(2,1)}, u32[]{:S(2)}) copy-start(bf16[2048,32]{0,1:T(8,128)(2,1)} %param.11) | copy-start | bytes 393220
  26.0 6.5 %copy-start.5 = (s32[4,2]{0,1:T(2,128)S(1)}, s32[4,2]{0,1:T(2,128)}, u32[]{:S(2)}) copy-start(s32[4,2]{0,1:T(2,128)} %param.14) | copy-start | bytes 100
  26.0 111.2 %all-to-all-start = ((bf16[4,256,3,768]{3,1,2,0:T(8,128)(2,1)}), bf16[4,256,3,768]{3,1,2,0:T(8,128)(2,1)}, u32[]{:S(2)}, u32[]{:S(2)}) async-start(bf16[4,256,3,768]{3,1,2,0:T(8,128)(2,1)} %select_select_fusion), calls=%async_computation | async-start | bytes 9437184 | tf_op jit(solution)/shard_map/all_to_all | solution.py:54
  145.3 5.2 %copy-start.1 = (bf16[128,2048]{1,0:T(8,128)(2,1)S(1)}, bf16[128,2048]{1,0:T(8,128)(2,1)}, u32[]{:S(2)}) copy-start(bf16[128,2048]{1,0:T(8,128)(2,1)} %param.8) | copy-start | bytes 1572868
  145.3 5.4 %copy-start.4 = (f32[2048]{0:T(1024)S(1)}, f32[2048]{0:T(1024)}, u32[]{:S(2)}) copy-start(f32[2048]{0:T(1024)} %param.10) | copy-start | bytes 24580
  145.3 110.5 %all-to-all-start.1 = ((bf16[8,256,3,768]{3,1,2,0:T(8,128)(2,1)}), bf16[8,256,3,768]{3,1,2,0:T(8,128)(2,1)}, u32[]{:S(2)}, u32[]{:S(2)}) async-start(bf16[8,256,3,768]{3,1,2,0:T(8,128)(2,1)} %bitcast.92), calls=%async_computation.1 | async-start | bytes 18874368 | tf_op jit(solution)/shard_map/all_to_all | solution.py:73
  150.9 113.1 %copy-start.3 = (bf16[128,2048]{1,0:T(8,128)(2,1)}, bf16[128,2048]{1,0:T(8,128)(2,1)S(1)}, u32[]{:S(2)}) copy-start(bf16[128,2048]{1,0:T(8,128)(2,1)S(1)} %fusion.17) | copy-start | bytes 1572868
  150.9 113.1 %collective-permute-start = (bf16[128,2048]{1,0:T(8,128)(2,1)S(1)}, bf16[128,2048]{1,0:T(8,128)(2,1)S(1)}, u32[]{:S(2)}, u32[]{:S(2)}) collective-permute-start(bf16[128,2048]{1,0:T(8,128)(2,1)S(1)} %fusion.17), channel_id=1, source_target_pairs={{0,4},{4,0},{8,12},{12,8},{16,20},{20,16},{24,28},{28,24},{1,5},{5... | collective-permute-start | bytes 1572872 | tf_op jit(solution)/shard_map/ppermute | solution.py:12
  268.6 3.5 %copy-start.7 = (f32[256,2,768]{2,0,1:T(8,128)}, f32[256,2,768]{2,0,1:T(8,128)S(1)}, u32[]{:S(2)}) copy-start(f32[256,2,768]{2,0,1:T(8,128)S(1)} %fusion.2) | copy-start | bytes 4718596
  272.1 2.1 copy-start.2
  272.1 2.5 copy-start.6
  272.2 2.0 collective-permute-start.1
  274.9 2.1 collective-permute-start.2
  285.0 2.0 collective-permute-start.3
where the time goes:
time: 290 us; the launch traced here: 289 us
  waiting for transfers between devices  212 us (73%)
  local copies, waits for them, and re-layouts  28.6 us (10%)
  matrix products  18 us (6%)
  other arithmetic  16.6 us (6%)
  starting transfers between devices  13.1 us (5%)
    all_to_all x1, waiting for transfers between devices, body(): lax.all_to_all(outgoing, 'expert', split_axis=0, concat_axis=0, tiled=True)  105 us
    all_to_all x1, waiting for transfers between devices, body(): lax.all_to_all(spread_out, 'dp', split_axis=0, concat_axis=1, tiled=True)[0]  104 us
    all_to_all x1, local copies, waits for them, and re-layouts, body(): lax.all_to_all(spread_out, 'dp', split_axis=0, concat_axis=1, tiled=True)[0]  8.21 us
    another operation x1, other arithmetic, body(): jnp.stack([gate_up_weight[:, :, :width], gate_up_weight[:, :, width:], do...  6.99 us
    gather x1, local copies, waits for them, and re-layouts, body(): jnp.take(owned, local_pick, axis=0)  6.77 us
    all_to_all x1, starting transfers between devices, body(): lax.all_to_all(outgoing, 'expert', split_axis=0, concat_axis=0, tiled=True)  6.45 us
  transfers between devices with their start and end apart: 6, of which 4 were waited for; matrix products, arithmetic and copies ran while one was open for 4% of the time, Pallas kernels for 0%

commit v1 on v0

--- a/solution.py
+++ b/solution.py
@@ -4,6 +4,22 @@
 from jax.sharding import PartitionSpec as P
 
 eps = 1e-05
+
+
+def pairwise_exchange(x, axis, split, join):
+    ways, here = (lax.axis_size(axis), lax.axis_index(axis))
+    width = x.shape[split] // ways
+    lengths = list(x.shape)
+    lengths[split] = width
+    height = lengths[join]
+    lengths[join] = height * ways
+    full = jnp.zeros(lengths, x.dtype)
+    for mask in range(ways):
+        part = lax.dynamic_slice_in_dim(x, (here ^ mask) * width, width, axis=split)
+        if mask:
+            part = lax.ppermute(part, axis, [(d, d ^ mask) for d in range(ways)])
+        full = lax.dynamic_update_slice_in_dim(full, part, (here ^ mask) * height, axis=join)
+    return full
 
 
 def partner(value, axis, stride):
@@ -51,7 +67,7 @@
         jnp.take(owned, local_pick, axis=0),
         jnp.zeros((), jnp.bfloat16),
     )
-    arrived = lax.all_to_all(outgoing, "expert", split_axis=0, concat_axis=0, tiled=True)
+    arrived = pairwise_exchange(outgoing, "expert", 0, 0)
     slot_rows = jnp.take(arrived, listed // held, axis=0)
     spread_out = jnp.broadcast_to(slot_rows[None], (ranks // 2,) + slot_rows.shape).reshape(
         (ranks,) + slot_rows.shape[1:]

time: 290 us -> 287 us (0.990)
  the two profiles are of different devices: /device:TPU:0 before, /device:TPU:17 now
where the time goes in v1:
time: 287 us; the launch traced here: 286 us
  waiting for transfers between devices  203 us (71%)
  local copies, waits for them, and re-layouts  35.9 us (13%)
  matrix products  18 us (6%)
  other arithmetic  14.4 us (5%)
  starting transfers between devices  14 us (5%)
    all_to_all x1, waiting for transfers between devices, body(): lax.all_to_all(spread_out, 'dp', split_axis=0, concat_axis=1, tiled=True)[0]  101 us
    ppermute x3, waiting for transfers between devices, pairwise_exchange(): part = lax.ppermute(part, axis, [(d, d ^ mask) for d in range(ways)])  98.5 us
    all_to_all x1, local copies, waits for them, and re-layouts, body(): lax.all_to_all(spread_out, 'dp', split_axis=0, concat_axis=1, tiled=True)[0]  8.21 us
    another operation x1, other arithmetic, body(): jnp.stack([gate_up_weight[:, :, :width], gate_up_weight[:, :, width:], do...  6.96 us
    all_to_all x1, starting transfers between devices, body(): lax.all_to_all(spread_out, 'dp', split_axis=0, concat_axis=1, tiled=True)[0]  6.88 us
    gather x1, local copies, waits for them, and re-layouts, body(): jnp.take(owned, local_pick, axis=0)  6.76 us
  transfers between devices with their start and end apart: 8, of which 6 were waited for; matrix products, arithmetic and copies ran while one was open for 5% of the time, Pallas kernels for 0%

profile of v1, /device:TPU:17, one launch (start us, length us, event | category | flops | bytes accessed | tf_op | source)
XLA Modules:
  0.0 286.2 jit_solution(1757520037420373830)
XLA Ops:
  0.6 0.7 fusion.65
  1.4 0.7 fusion.50
  2.1 5.0 %slice_bitcast_fusion.2 = (bf16[8,256,1,768]{3,1,0,2:T(8,128)(2,1)S(1)}, bf16[8,256,1,768]{3,1,0,2:T(8,128)(2,1)}) fusion(bf16[8,256,1536]{2,1,0:T(8,128)(2,1)} %param.12), kind=kLoop, calls=%fused_computation.11 | loop fusion | bytes 12582912 | tf_op jit(solution)/shard_map/stack | solution.py:62
  7.1 7.0 %pad_maximum_fusion = bf16[8,256,3,768]{3,1,0,2:T(8,128)(2,1)} fusion(bf16[8,256,1,768]{3,1,0,2:T(8,128)(2,1)} %bitcast.97, bf16[8,256,1,768]{3,1,0,2:T(8,128)(2,1)} %get-tuple-element.9, bf16[8,256,1,768]{3,1,0,2:T(8,128)(2,1)S(1)} %get-tuple-element.8), kind=kLoop, calls=%fused_computation.3 | loop fusion | flops 9437184 | bytes 18874368 | tf_op jit(solution)/shard_map/stack | solution.py:62
  14.1 6.8 %gather_fusion.1 = bf16[4,256,3,768]{3,1,2,0:T(8,128)(2,1)} fusion(bf16[8,256,3,768]{3,1,0,2:T(8,128)(2,1)} %pad_maximum_fusion, s32[1024]{0:T(1024)S(1)} %pad_clamp_fusion.1), kind=kCustom, calls=%fused_computation.1 | custom fusion | bytes 9437200 | tf_op jit(solution)/shard_map/jit(_take)/gather | solution.py:67
  20.9 2.9 %select_select_fusion = bf16[4,256,3,768]{3,1,2,0:T(8,128)(2,1)S(1)} fusion(bf16[4,256,3,768]{3,1,2,0:T(8,128)(2,1)} %gather_fusion.1, pred[4]{0:T(512)(128)(4,1)S(1)} %compare_and_fusion, pred[4]{0:T(512)(128)(4,1)S(1)} %get-tuple-element.6), kind=kLoop, calls=%fused_computation.8 | loop fusion | flops 4718592 | bytes 9437192 | tf_op jit(solution)/shard_map/jit(_where)/select_n | solution.py:65
  23.8 2.5 broadcast_in_dim.65
  26.3 1.4 constant_dynamic-slice_fusion.1
  27.7 1.3 collective-permute-start.1
  29.0 1.3 collective-permute-start.3
  30.6 47.0 %collective-permute-done.1 = bf16[1,256,3,768]{3,1,2,0:T(8,128)(2,1)S(1)} collective-permute-done((bf16[1,256,3,768]{3,1,2,0:T(8,128)(2,1)S(1)}, bf16[1,256,3,768]{3,1,2,0:T(8,128)(2,1)S(1)}, u32[]{:S(2)}, u32[]{:S(2)}) %collective-permute-start.1) | collective-permute-done | bytes 1179680 | tf_op jit(solution)/shard_map/ppermute | solution.py:20
  77.6 1.1 constant_dynamic-update-slice_fusion.2
  78.7 1.1 collective-permute-done.2
  79.7 1.1 constant_dynamic-update-slice_fusion.1
  80.8 50.5 %collective-permute-done.3 = bf16[1,256,3,768]{3,1,2,0:T(8,128)(2,1)S(1)} collective-permute-done((bf16[1,256,3,768]{3,1,2,0:T(8,128)(2,1)S(1)}, bf16[1,256,3,768]{3,1,2,0:T(8,128)(2,1)S(1)}, u32[]{:S(2)}, u32[]{:S(2)}) %collective-permute-start.3) | collective-permute-done | bytes 1179680 | tf_op jit(solution)/shard_map/ppermute | solution.py:20
  131.3 1.1 constant_dynamic-update-slice_fusion
  132.4 3.0 %gather_fusion.2 = bf16[2,256,3,768]{3,1,2,0:T(8,128)(2,1)S(1)} fusion(bf16[4,256,3,768]{3,1,2,0:T(8,128)(2,1)} %constant_dynamic-update-slice_fusion, s32[1024]{0:T(1024)S(1)} %pad_clamp_fusion), kind=kCustom, calls=%fused_computation.2 | custom fusion | bytes 4718600 | tf_op jit(solution)/shard_map/jit(_take)/gather | solution.py:71
  135.7 4.7 %broadcast_in_dim.70 = bf16[4,2,256,3,768]{4,2,3,1,0:T(8,128)(2,1)} broadcast(bf16[2,256,3,768]{3,1,2,0:T(8,128)(2,1)S(1)} %broadcast_select_fusion), dimensions={1,2,3,4} | broadcast | bytes 11796480 | tf_op jit(solution)/shard_map/broadcast_in_dim | solution.py:72
  140.5 6.9 %all-to-all-start = ((bf16[8,256,3,768]{3,1,2,0:T(8,128)(2,1)}), bf16[8,256,3,768]{3,1,2,0:T(8,128)(2,1)}, u32[]{:S(2)}, u32[]{:S(2)}) async-start(bf16[8,256,3,768]{3,1,2,0:T(8,128)(2,1)} %bitcast.92), calls=%async_computation | async-start | bytes 18874368 | tf_op jit(solution)/shard_map/all_to_all | solution.py:89
  148.2 100.9 %all-to-all-done = bf16[8,256,3,768]{3,1,2,0:T(8,128)(2,1)} async-done(((bf16[8,256,3,768]{3,1,2,0:T(8,128)(2,1)}), bf16[8,256,3,768]{3,1,2,0:T(8,128)(2,1)}, u32[]{:S(2)}, u32[]{:S(2)}) %all-to-all-start) | async-done | bytes 9437216 | tf_op jit(solution)/shard_map/all_to_all | solution.py:89
  249.1 8.2 %copy.11 = bf16[8,256,3,768]{3,1,0,2:T(8,128)(2,1)} copy(bf16[8,256,3,768]{3,1,2,0:T(8,128)(2,1)} %all-to-all-done) | data formatting | bytes 18874368 | tf_op jit(solution)/shard_map/all_to_all | solution.py:89
  257.3 4.6 %fusion.2 = f32[256,2,768]{2,0,1:T(8,128)S(1)} fusion(bf16[2048,3,768]{2,0,1:T(8,128)(2,1)} %bitcast.93, bf16[128,2048]{1,0:T(8,128)(2,1)S(1)} %collective-permute-done, bf16[128,2048]{1,0:T(8,128)(2,1)S(1)} %fusion.17), kind=kOutput, calls=%fused_computation.6 | convolution fusion | flops 1612709888 | bytes 8912896 | tf_op jit(solution)/shard_map/td,dkf->tkf/dot_general | solution.py:90
  261.9 3.5 %fusion.12 = bf16[256,2048]{1,0:T(8,128)(2,1)S(1)} fusion(bf16[2048,3,768]{2,0,1:T(8,128)(2,1)} %bitcast.94, f32[256,2,768]{2,0,1:T(8,128)S(1)} %fusion.2), kind=kOutput, calls=%fused_computation.16 | convolution fusion | flops 807010304 | bytes 5767168 | tf_op jit(solution)/shard_map/tf,df->td/dot_general | solution.py:98
  265.5 3.8 %collective-permute-start.4 = (bf16[128,2048]{1,0:T(8,128)(2,1)S(1)}, bf16[128,2048]{1,0:T(8,128)(2,1)S(1)}, u32[]{:S(2)}, u32[]{:S(2)}) collective-permute-start(bf16[128,2048]{1,0:T(8,128)(2,1)S(1)} %slice.53), channel_id=1, source_target_pairs={{0,4},{4,0},{8,12},{12,8},{16,20},{20,16},{24,28},{28,24},{1,5},{5... | collective-permute-start | bytes 1572872 | tf_op jit(solution)/shard_map/ppermute | solution.py:28
  269.3 0.6 gather_fusion
  269.8 1.3 fusion.64
  271.9 1.9 collective-permute-done.5
  273.8 3.4 %fusion.45 = (bf16[256,1,768]{2,0,1:T(8,128)(2,1)S(1)}, bf16[256,1,768]{2,0,1:T(8,128)(2,1)S(1)}) fusion(f32[256,2,768]{2,0,1:T(8,128)} %copy-done.7, bf16[2048,3,768]{2,0,1:T(8,128)(2,1)} %bitcast.95, bf16[128,2048]{1,0:T(8,128)(2,1)S(1)} %collective-permute-done.5, bf16[128,2048]{1,0:T(8,128)(2,1)S(1)} %get-tuple-element.18), kind=kOutput, calls=%fused_computation.70 | convolution fusion | flops 809959424 | bytes 6553600 | tf_op jit(solution)/shard_map/td,df->tf/dot_general | solution.py:117
  277.3 4.6 %fusion.9 = bf16[256,2048]{1,0:T(8,128)(2,1)S(1)} fusion(bf16[2048,3,768]{2,0,1:T(8,128)(2,1)} %bitcast.96, bf16[256,1,768]{2,0,1:T(8,128)(2,1)S(1)} %get-tuple-element.15, bf16[256,1,768]{2,0,1:T(8,128)(2,1)S(1)} %get-tuple-element.14), kind=kOutput, calls=%fused_computation.15 | convolution fusion | flops 1611530240 | bytes 8126464 | tf_op jit(solution)/shard_map/tkf,dkf->td/dot_general | solution.py:124
  282.1 1.8 collective-permute-done.6
  283.9 0.5 fusion.20
  284.5 1.7 fusion.25
  (43 shorter events, 2.4 us)
Async XLA Ops:
  0.6 268.6 %copy-start = (bf16[2048,32]{0,1:T(8,128)(2,1)S(1)}, bf16[2048,32]{0,1:T(8,128)(2,1)}, u32[]{:S(2)}) copy-start(bf16[2048,32]{0,1:T(8,128)(2,1)} %param.11) | copy-start | bytes 393220
  26.3 4.0 %copy-start.5 = (s32[4,2]{0,1:T(2,128)S(1)}, s32[4,2]{0,1:T(2,128)}, u32[]{:S(2)}) copy-start(s32[4,2]{0,1:T(2,128)} %param.14) | copy-start | bytes 100
  27.7 49.9 %collective-permute-start.1 = (bf16[1,256,3,768]{3,1,2,0:T(8,128)(2,1)S(1)}, bf16[1,256,3,768]{3,1,2,0:T(8,128)(2,1)S(1)}, u32[]{:S(2)}, u32[]{:S(2)}) collective-permute-start(bf16[1,256,3,768]{3,1,2,0:T(8,128)(2,1)S(1)} %get-tuple-element.12), channel_id=1, source_target_pairs={{0,1},{1,0},{2,3},{3,2},{4,5},{5,4},{6,7},{7,6},{8,9},{9,8},{10,11... | collective-permute-start | bytes 3538952 | tf_op jit(solution)/shard_map/ppermute | solution.py:20
  29.0 50.7 %collective-permute-start.2 = (bf16[1,256,3,768]{3,1,2,0:T(8,128)(2,1)S(1)}, bf16[1,256,3,768]{3,1,2,0:T(8,128)(2,1)S(1)}, u32[]{:S(2)}, u32[]{:S(2)}) collective-permute-start(bf16[1,256,3,768]{3,1,2,0:T(8,128)(2,1)S(1)} %get-tuple-element.11), channel_id=1, source_target_pairs={{0,2},{1,3},{2,0},{3,1},{4,6},{5,7},{6,4},{7,5},{8,10},{9,11},{10,... | collective-permute-start | bytes 3538952 | tf_op jit(solution)/shard_map/ppermute | solution.py:20
  29.0 102.3 %collective-permute-start.3 = (bf16[1,256,3,768]{3,1,2,0:T(8,128)(2,1)S(1)}, bf16[1,256,3,768]{3,1,2,0:T(8,128)(2,1)S(1)}, u32[]{:S(2)}, u32[]{:S(2)}) collective-permute-start(bf16[1,256,3,768]{3,1,2,0:T(8,128)(2,1)S(1)} %get-tuple-element.10), channel_id=1, source_target_pairs={{0,3},{1,2},{2,1},{3,0},{4,7},{5,6},{6,5},{7,4},{8,11},{9,10},{10,... | collective-permute-start | bytes 3538952 | tf_op jit(solution)/shard_map/ppermute | solution.py:20
  140.5 6.9 %copy-start.1 = (bf16[128,2048]{1,0:T(8,128)(2,1)S(1)}, bf16[128,2048]{1,0:T(8,128)(2,1)}, u32[]{:S(2)}) copy-start(bf16[128,2048]{1,0:T(8,128)(2,1)} %param.8) | copy-start | bytes 1572868
  140.5 7.1 %copy-start.4 = (f32[2048]{0:T(1024)S(1)}, f32[2048]{0:T(1024)}, u32[]{:S(2)}) copy-start(f32[2048]{0:T(1024)} %param.10) | copy-start | bytes 24580
  140.5 108.6 %all-to-all-start = ((bf16[8,256,3,768]{3,1,2,0:T(8,128)(2,1)}), bf16[8,256,3,768]{3,1,2,0:T(8,128)(2,1)}, u32[]{:S(2)}, u32[]{:S(2)}) async-start(bf16[8,256,3,768]{3,1,2,0:T(8,128)(2,1)} %bitcast.92), calls=%async_computation | async-start | bytes 18874368 | tf_op jit(solution)/shard_map/all_to_all | solution.py:89
  147.8 109.5 %copy-start.3 = (bf16[128,2048]{1,0:T(8,128)(2,1)}, bf16[128,2048]{1,0:T(8,128)(2,1)S(1)}, u32[]{:S(2)}) copy-start(bf16[128,2048]{1,0:T(8,128)(2,1)S(1)} %fusion.17) | copy-start | bytes 1572868
  147.8 109.5 %collective-permute-start = (bf16[128,2048]{1,0:T(8,128)(2,1)S(1)}, bf16[128,2048]{1,0:T(8,128)(2,1)S(1)}, u32[]{:S(2)}, u32[]{:S(2)}) collective-permute-start(bf16[128,2048]{1,0:T(8,128)(2,1)S(1)} %fusion.17), channel_id=1, source_target_pairs={{0,4},{4,0},{8,12},{12,8},{16,20},{20,16},{24,28},{28,24},{1,5},{5... | collective-permute-start | bytes 1572872 | tf_op jit(solution)/shard_map/ppermute | solution.py:28
  261.9 3.5 %copy-start.7 = (f32[256,2,768]{2,0,1:T(8,128)}, f32[256,2,768]{2,0,1:T(8,128)S(1)}, u32[]{:S(2)}) copy-start(f32[256,2,768]{2,0,1:T(8,128)S(1)} %fusion.2) | copy-start | bytes 4718596
  265.4 5.8 %copy-start.2 = (bf16[128,2048]{1,0:T(8,128)(2,1)S(1)}, bf16[128,2048]{1,0:T(8,128)(2,1)}, u32[]{:S(2)}) copy-start(bf16[128,2048]{1,0:T(8,128)(2,1)} %param.9) | copy-start | bytes 1572868
  265.4 6.2 %copy-start.6 = (s32[128,1]{0,1:T(1,128)S(1)}, s32[128,1]{0,1:T(1,128)}, u32[]{:S(2)}) copy-start(s32[128,1]{0,1:T(1,128)} %param.15) | copy-start | bytes 1540
  265.5 5.7 %collective-permute-start.4 = (bf16[128,2048]{1,0:T(8,128)(2,1)S(1)}, bf16[128,2048]{1,0:T(8,128)(2,1)S(1)}, u32[]{:S(2)}, u32[]{:S(2)}) collective-permute-start(bf16[128,2048]{1,0:T(8,128)(2,1)S(1)} %slice.53), channel_id=1, source_target_pairs={{0,4},{4,0},{8,12},{12,8},{16,20},{20,16},{24,28},{28,24},{1,5},{5... | collective-permute-start | bytes 1572872 | tf_op jit(solution)/shard_map/ppermute | solution.py:28
  271.8 2.0 collective-permute-start.5
  281.9 2.0 collective-permute-start.6
